TPU v7x, 32 devices: a whole 2x2x4 slice. The times are simulated.
32 devices in a mesh: expert: 4 (over x, core), context: 2 (over y), dp: 4 (over z).
Axes of the slice: x: 2, y: 2, z: 4, core: 2. Of those that a mesh axis runs over, the one named last changes fastest.
Arguments:
- tokens: bfloat16 [16, 512, 1024], P(('expert', 'dp'), 'context'), may hold values from -6 to 6
- span_order: int32 [4], replicated, may hold values from 0 to 3, each once
- routes: int32 [16, 512, 8], P(('expert', 'dp'), 'context'), may hold values from 0 to 15, all different within a row; in each aligned block of 256 rows (0 to 255, 256 to 511, ..., all dimensions but the last counted through in order) at most 160 rows name the same one
- norm_attn: bfloat16 [1024], replicated, may hold values from 0.5 to 1.5
- w_query: bfloat16 [1024, 1024], replicated, may hold values from -0.1875 to 0.1875
- w_key: bfloat16 [1024, 512], replicated, may hold values from -0.1875 to 0.1875
- w_value: bfloat16 [1024, 512], replicated, may hold values from -0.1875 to 0.1875
- w_out: bfloat16 [1024, 1024], replicated, may hold values from -1.5 to 1.5
- norm_moe: bfloat16 [1024], replicated, may hold values from 0.5 to 1.5
- w_router: bfloat16 [1024, 16], replicated, may hold values from -0.09375 to 0.09375
- w_gate: bfloat16 [16, 1024, 512], P('expert'), may hold values from -0.1875 to 0.1875
- w_up: bfloat16 [16, 1024, 512], P('expert'), may hold values from -0.1875 to 0.1875
- w_down: bfloat16 [16, 512, 1024], P('expert'), may hold values from -1 to 1
- cotangent: bfloat16 [16, 512, 1024], P(('expert', 'dp'), 'context'), may hold values from -6 to 6
Outputs:
- outputs: bfloat16 [16, 512, 1024], P(('expert', 'dp'), 'context')
- grad_tokens: bfloat16 [16, 512, 1024], P(('expert', 'dp'), 'context')
- grad_norm_attn: float32 [1024], replicated
- grad_query: float32 [1024, 1024], replicated
- grad_key: float32 [1024, 512], replicated
- grad_value: float32 [1024, 512], replicated
- grad_out: float32 [1024, 1024], replicated
- grad_norm_moe: float32 [1024], replicated
- grad_router: float32 [1024, 16], replicated
- grad_gate: float32 [16, 1024, 512], P('expert')
- grad_up: float32 [16, 1024, 512], P('expert')
- grad_down: float32 [16, 512, 1024], P('expert')
Inputs may be any that keep to these rules, and one draw needn't show every extreme that they name: span_order is a permutation; stored block j of every sequence holds the tokens at positions span_order[j] * 128 to span_order[j] * 128 + 127. `routes`: each token names 8 different experts. Within the rows of one device (aligned blocks of 256 rows, in order), no expert is named by more than 160 rows, a bound that some block reaches.
All inputs are finite; a program needn't handle non-finite values.
Results may differ from a plain program's by a relative error of at most 0.017.
Values may be sent and summed in bfloat16 or wider, within the bound.
A program may use at most 192 MiB of HBM per device.

v0:
```python
import math
import jax
import jax.numpy as jnp
from jax import lax
from jax.sharding import PartitionSpec as P

H = 16
KV = 8
HD = 64
EXPERTS = 16
SPAN = 128
EPSILON = 1e-06
ROPE_BASE = 10000.0
MASKED = -1e30
F32 = jnp.float32
BF16 = jnp.bfloat16


def rope_tables(positions):
    half_dim = HD // 2
    frequency = ROPE_BASE ** (-(jnp.arange(half_dim, dtype=F32) * 2.0) / HD)
    angles = positions.astype(F32)[:, None] * frequency[None, :]
    return (jnp.cos(angles), jnp.sin(angles))


def rotate(tensor, cos_table, sin_table):
    half_dim = tensor.shape[-1] // 2
    front = tensor[..., :half_dim]
    back = tensor[..., half_dim:]
    cos_wide = cos_table[:, None, :]
    sin_wide = sin_table[:, None, :]
    return jnp.concatenate(
        [front * cos_wide - back * sin_wide, back * cos_wide + front * sin_wide], axis=-1
    )


def positions_of(row_index, span_order):
    block_ids = row_index // SPAN
    picked = jnp.where(
        block_ids[:, None] == jnp.arange(span_order.shape[0], dtype=jnp.int32)[None, :],
        span_order[None, :],
        0,
    )
    return jnp.sum(picked, axis=1, dtype=jnp.int32) * SPAN + row_index % SPAN


def norm_back(grad_normed, normed, inv_root):
    return inv_root * (
        grad_normed - normed * jnp.mean(grad_normed * normed, axis=-1, keepdims=True)
    )


def dot(a, b):
    return jnp.dot(a, b, preferred_element_type=F32)


def dot_t(a, b):
    return lax.dot_general(a, b, (((1,), (1,)), ((), ())), preferred_element_type=F32)


def t_dot(a, b):
    return lax.dot_general(a, b, (((0,), (0,)), ((), ())), preferred_element_type=F32)


def body(
    tokens,
    span_order,
    routes,
    norm_attn,
    w_query,
    w_key,
    w_value,
    w_out,
    norm_moe,
    w_router,
    w_gate,
    w_up,
    w_down,
    cotangent,
):
    tok_rows = tokens.shape[1]
    width = tokens.shape[2]
    seq_rows = tok_rows * lax.axis_size("context")
    groups = H // KV
    score_scale = 1.0 / math.sqrt(HD)
    local_experts = w_gate.shape[0]
    ff = w_gate.shape[2]
    dy_all = lax.all_gather(cotangent[0], "expert", axis=0, tiled=True)
    routes_all = lax.all_gather(routes[0], "expert", axis=0, tiled=True)
    local_index = lax.axis_index("context") * tok_rows + jnp.arange(tok_rows, dtype=jnp.int32)
    pos_query = positions_of(local_index, span_order)
    pos_keys = positions_of(jnp.arange(seq_rows, dtype=jnp.int32), span_order)
    cos_table, sin_table = rope_tables(pos_query)
    allowed = pos_keys[None, :] <= pos_query[:, None]
    inputs = tokens[0].astype(F32)
    inv_one = lax.rsqrt(jnp.mean(inputs * inputs, axis=-1, keepdims=True) + EPSILON)
    normed_one = inputs * inv_one
    gain_one = norm_attn.astype(F32)
    h_one = (normed_one * gain_one).astype(BF16)
    key_pre = dot(h_one, w_key).reshape(tok_rows, KV, HD)
    keys_local = rotate(key_pre, cos_table, sin_table).astype(BF16).reshape(tok_rows, KV * HD)
    values_local = dot(h_one, w_value).astype(BF16)
    kv_all = lax.all_gather(
        jnp.concatenate([keys_local, values_local], axis=1), "context", axis=0, tiled=True
    )
    query_pre = dot(h_one, w_query).reshape(tok_rows, H, HD)
    queries = rotate(query_pre, cos_table, sin_table).astype(BF16).reshape(tok_rows, KV, groups, HD)
    keys_all = kv_all[:, : KV * HD].reshape(seq_rows, KV, HD)
    values_all = kv_all[:, KV * HD :].reshape(seq_rows, KV, HD)
    scores = (
        jnp.einsum("qkgd,skd->kgqs", queries, keys_all, preferred_element_type=F32) * score_scale
    )
    masked = jnp.where(allowed, scores, MASKED)
    top_score = jnp.max(masked, axis=-1, keepdims=True)
    exp_scores = jnp.exp(masked - top_score)
    total_exp = jnp.sum(exp_scores, axis=-1, keepdims=True)
    attn_probs = exp_scores / total_exp
    probs_rounded = attn_probs.astype(BF16)
    mixed_heads = jnp.einsum(
        "kgqs,skd->qkgd", probs_rounded, values_all, preferred_element_type=F32
    )
    mixed_heads = mixed_heads.reshape(tok_rows, H * HD).astype(BF16)
    y_one = inputs + dot(mixed_heads, w_out)
    inv_two = lax.rsqrt(jnp.mean(y_one * y_one, axis=-1, keepdims=True) + EPSILON)
    normed_two = y_one * inv_two
    gain_two = norm_moe.astype(F32)
    h_two = (normed_two * gain_two).astype(BF16)
    h_all = lax.all_gather(h_two, "expert", axis=0, tiled=True)
    experts = jnp.arange(EXPERTS, dtype=jnp.int32)
    chosen = jnp.any(routes_all[:, :, None] == experts[None, None, :], axis=1)
    logits = jnp.where(chosen, dot(h_all, w_router), MASKED)
    weights = jnp.where(chosen, jnp.exp(logits - jnp.max(logits, axis=-1, keepdims=True)), 0.0)
    weights = weights / jnp.sum(weights, axis=-1, keepdims=True)
    me = lax.axis_index("expert")
    mine = lax.dynamic_slice_in_dim(weights, me * local_experts, local_experts, axis=1)
    partial_y = None
    partial_h = None
    dots = []
    g_gate, g_up, g_down = ([], [], [])
    for e in range(local_experts):
        weight = mine[:, e : e + 1]
        gate_pre = dot(h_all, w_gate[e])
        upward = dot(h_all, w_up[e])
        back = dot_t(dy_all, w_down[e])
        sigmoid_gate = jax.nn.sigmoid(gate_pre)
        silu_gate = gate_pre * sigmoid_gate
        hidden = silu_gate * upward
        hidden_w = (hidden * weight).astype(BF16)
        dots.append(jnp.sum(hidden * back, axis=-1, keepdims=True))
        grad_hidden = back * weight
        grad_gate_pre = (
            grad_hidden * upward * sigmoid_gate * (1.0 + gate_pre * (1.0 - sigmoid_gate))
        ).astype(BF16)
        grad_up_pre = (grad_hidden * silu_gate).astype(BF16)
        add_y = dot(hidden_w, w_down[e])
        add_h = dot_t(grad_gate_pre, w_gate[e]) + dot_t(grad_up_pre, w_up[e])
        partial_y = add_y if partial_y is None else partial_y + add_y
        partial_h = add_h if partial_h is None else partial_h + add_h
        g_down.append(t_dot(hidden_w, dy_all).astype(BF16))
        g_gate.append(t_dot(h_all, grad_gate_pre).astype(BF16))
        g_up.append(t_dot(h_all, grad_up_pre).astype(BF16))
    d_weights = jnp.concatenate(dots, axis=1)
    d_wide = lax.dynamic_update_slice_in_dim(
        jnp.zeros((d_weights.shape[0], EXPERTS), F32), d_weights, me * local_experts, axis=1
    )
    d_high = lax.reduce_precision(d_wide, 8, 7)
    packed = jnp.concatenate(
        [
            partial_h.astype(BF16),
            d_high.astype(BF16),
            (d_wide - d_high).astype(BF16),
            jnp.zeros((d_wide.shape[0], 128 - 2 * EXPERTS), BF16),
        ],
        axis=1,
    )
    home = lax.psum_scatter(packed, "expert", scatter_dimension=0, tiled=True).astype(F32)
    y_two = lax.psum_scatter(
        partial_y.astype(BF16), "expert", scatter_dimension=0, tiled=True
    ).astype(F32)
    total_gate, total_up, total_down = (
        lax.psum(jnp.stack(g), ("context", "dp")).astype(F32) for g in (g_gate, g_up, g_down)
    )
    outputs = (y_one + y_two).astype(BF16)[None]
    grad_final = cotangent[0].astype(F32)
    grad_weights = home[:, width : width + EXPERTS] + home[:, width + EXPERTS : width + 2 * EXPERTS]
    own = lax.dynamic_slice_in_dim(weights, me * tok_rows, tok_rows, axis=0)
    grad_logits = (
        own * (grad_weights - jnp.sum(own * grad_weights, axis=-1, keepdims=True))
    ).astype(BF16)
    grad_router_w = t_dot(h_two, grad_logits)
    grad_h_two = home[:, :width] + dot_t(grad_logits, w_router)
    grad_gain_two = jnp.sum(grad_h_two * normed_two, axis=0)
    grad_y_one = grad_final + norm_back(grad_h_two * gain_two, normed_two, inv_two)
    grad_attn = grad_y_one.astype(BF16)
    grad_out_w = t_dot(mixed_heads, grad_attn)
    grad_mixed = dot_t(grad_attn, w_out).astype(BF16).reshape(tok_rows, KV, groups, HD)
    grad_probs = jnp.einsum("qkgd,skd->kgqs", grad_mixed, values_all, preferred_element_type=F32)
    grad_values = jnp.einsum(
        "kgqs,qkgd->skd", probs_rounded, grad_mixed, preferred_element_type=F32
    )
    row_dots = jnp.sum(attn_probs * grad_probs, axis=-1, keepdims=True)
    grad_scores = (attn_probs * (grad_probs - row_dots)).astype(BF16)
    grad_keys = (
        jnp.einsum("kgqs,qkgd->skd", grad_scores, queries, preferred_element_type=F32) * score_scale
    )
    grad_kv = lax.psum_scatter(
        jnp.concatenate(
            [grad_keys.reshape(seq_rows, KV * HD), grad_values.reshape(seq_rows, KV * HD)], axis=1
        ).astype(BF16),
        "context",
        scatter_dimension=0,
        tiled=True,
    ).astype(F32)
    grad_queries = (
        jnp.einsum("kgqs,skd->qkgd", grad_scores, keys_all, preferred_element_type=F32)
        * score_scale
    )
    grad_q_pre = (
        rotate(grad_queries.reshape(tok_rows, H, HD), cos_table, -sin_table)
        .reshape(tok_rows, H * HD)
        .astype(BF16)
    )
    grad_k_pre = (
        rotate(grad_kv[:, : KV * HD].reshape(tok_rows, KV, HD), cos_table, -sin_table)
        .reshape(tok_rows, KV * HD)
        .astype(BF16)
    )
    grad_v_pre = grad_kv[:, KV * HD :].astype(BF16)
    grad_query_w = t_dot(h_one, grad_q_pre)
    grad_key_w = t_dot(h_one, grad_k_pre)
    grad_value_w = t_dot(h_one, grad_v_pre)
    grad_h_one = dot_t(grad_q_pre, w_query) + dot_t(grad_k_pre, w_key) + dot_t(grad_v_pre, w_value)
    grad_gain_one = jnp.sum(grad_h_one * normed_one, axis=0)
    grad_inputs = grad_y_one + norm_back(grad_h_one * gain_one, normed_one, inv_one)
    grad_tokens = grad_inputs.astype(BF16)[None]
    everywhere = ("expert", "context", "dp")
    total_o = lax.psum(grad_out_w.astype(BF16), everywhere).astype(F32)
    total_q, total_k, total_v = (
        t.astype(F32)
        for t in lax.psum(
            tuple((g.astype(BF16) for g in (grad_query_w, grad_key_w, grad_value_w))), everywhere
        )
    )
    total_g1, total_g2, total_r = lax.psum(
        (grad_gain_one, grad_gain_two, grad_router_w), everywhere
    )
    return (
        outputs,
        grad_tokens,
        total_g1,
        total_q,
        total_k,
        total_v,
        total_o,
        total_g2,
        total_r,
        total_gate,
        total_up,
        total_down,
    )


def solution(mesh):
    in_specs = (
        P(("expert", "dp"), "context", None),
        P(),
        P(("expert", "dp"), "context", None),
        P(),
        P(),
        P(),
        P(),
        P(),
        P(),
        P(),
        P("expert", None, None),
        P("expert", None, None),
        P("expert", None, None),
        P(("expert", "dp"), "context", None),
    )
    out_specs = (
        P(("expert", "dp"), "context", None),
        P(("expert", "dp"), "context", None),
        P(),
        P(),
        P(),
        P(),
        P(),
        P(),
        P(),
        P("expert", None, None),
        P("expert", None, None),
        P("expert", None, None),
    )
    return jax.shard_map(body, mesh=mesh, in_specs=in_specs, out_specs=out_specs, check_vma=False)
```

profile of v0, /device:TPU:1, one launch (start us, length us, event | category | flops | bytes accessed | tf_op | source)
XLA Modules:
  0.0 959.9 jit_solution(15199929937461508150)
XLA Ops:
  19.1 3.9 copy.122
  27.2 14.6 %all-gather.6.cloned.1.call-done = bf16[512,1024]{1,0:T(8,128)(2,1)} async-done(((bf16[256,1024]{1,0:T(8,128)(2,1)}), bf16[512,1024]{1,0:T(8,128)(2,1)}) %all-gather.6.cloned.1.call-update) | async-done | bytes 1048592 | tf_op jit(solution)/shard_map/all_gather | solution.py:103
  46.1 8.0 fusion.203
  54.1 4.3 fusion.74
  61.6 6.1 all-gather
  67.9 4.6 fusion.16
  80.3 11.1 %all-gather.8.cloned.1.call-done = bf16[1024,1024]{0,1:T(8,128)(2,1)} async-done(((bf16[256,1024]{0,1:T(8,128)(2,1)}), bf16[1024,1024]{0,1:T(8,128)(2,1)}) %all-gather.8.cloned.1.call-update) | async-done | bytes 2097168 | tf_op jit(solution)/shard_map/all_gather | solution.py:128
  134.0 9.2 add_convert_fusion
  156.7 4.3 fusion.47
  167.9 11.0 %reduce-scatter.6.cloned.1.call-done = bf16[256,1152]{0,1:T(8,128)(2,1)} async-done(((bf16[1024,1152]{0,1:T(8,128)(2,1)}), bf16[256,1152]{0,1:T(8,128)(2,1)}) %reduce-scatter.6.cloned.1.call-update) | async-done | bytes 589840 | tf_op jit(solution)/shard_map/reduce_scatter | solution.py:176
  182.5 30.9 %reduce-scatter.4.cloned.1.call-done = bf16[256,1024]{0,1:T(8,128)(2,1)} async-done(((bf16[1024,1024]{0,1:T(8,128)(2,1)}), bf16[256,1024]{0,1:T(8,128)(2,1)}) %reduce-scatter.4.cloned.1.call-update) | async-done | bytes 524304 | tf_op jit(solution)/shard_map/reduce_scatter | solution.py:177
  218.9 4.9 fusion.1
  223.8 4.8 fusion.78
  228.6 4.5 fusion.3
  236.8 4.0 fusion.51
  249.7 7.0 reduce-scatter.8.cloned.1.call-done
  291.6 39.5 %all-reduce = (f32[1024]{0:T(1024)}, f32[1024]{0:T(1024)}) all-reduce(f32[1024]{0:T(1024)S(1)} %get-tuple-element.26, f32[1024]{0:T(1024)S(1)} %get-tuple-element.24), channel_id=1, replica_groups=mesh['expert'=4,'context'=2,'dp'=4] {'expert','context','dp'}, use_global_device_ids=true, to_apply=%region_21.22 | all-reduce | flops 2048 | bytes 16384 | tf_op jit(solution)/shard_map/psum | solution.py:244
  331.1 90.1 %all-reduce.9.cloned.1.call-done = (bf16[1024,1024]{1,0:T(8,128)(2,1)}, bf16[1024,512]{1,0:T(8,128)(2,1)}, bf16[1024,512]{1,0:T(8,128)(2,1)}, bf16[1024,1024]{1,0:T(8,128)(2,1)}) async-done(((bf16[1024,1024]{1,0:T(8,128)(2,1)}, bf16[1024,512]{1,0:T(8,128)(2,1)}, bf16[1024,512]{1,0:T(8,128)(2,1)}, bf16[1024,1024]{1,0:T(8,128)(2,1)}), (bf16[1024,1024]{1,0:T(8,128)(2,1)}, bf16[1024,512]{1,0:T(8,128)(2,1)}, ...) | async-done | bytes 6291472 | tf_op jit(solution)/shard_map/psum | solution.py:240
  421.2 4.2 convert_element_type.280
  431.8 394.5 %all-reduce.11.cloned.1.call-done = (bf16[4,1024,512]{2,1,0:T(8,128)(2,1)}, bf16[4,1024,512]{2,1,0:T(8,128)(2,1)}, bf16[4,512,1024]{2,1,0:T(8,128)(2,1)}) async-done(((bf16[4,1024,512]{2,1,0:T(8,128)(2,1)}, bf16[4,1024,512]{2,1,0:T(8,128)(2,1)}, bf16[4,512,1024]{2,1,0:T(8,128)(2,1)}), (bf16[4,1024,512]{2,1,0:T(8,128)(2,1)}, bf16[4,1024,512]{2,1,0:T(8,128)(2,1)}, ...) | async-done | bytes 12582928 | tf_op jit(solution)/shard_map/psum | solution.py:181
  826.2 6.9 convert_element_type.291
  833.1 4.6 convert_element_type.296
  837.7 4.4 convert_element_type.301
  842.2 109.5 %all-reduce.7.cloned.1.call-done = f32[1024,16]{0,1:T(8,128)} async-done(((f32[1024,16]{0,1:T(8,128)}), f32[1024,16]{0,1:T(8,128)}) %all-reduce.7.cloned.1.call-update) | async-done | bytes 65552 | tf_op jit(solution)/shard_map/psum | solution.py:244
  (304 shorter events, 157.8 us)
Async XLA Ops:
  7.2 51.3 %copy-start = (bf16[1024,1024]{1,0:T(8,128)(2,1)S(1)}, bf16[1024,1024]{1,0:T(8,128)(2,1)}, u32[]{:S(2)}) copy-start(bf16[1024,1024]{1,0:T(8,128)(2,1)} %param.21) | copy-start | bytes 6291460
  7.2 34.6 %all-gather.6.cloned.1.call-start = ((), (), s32[]{:S(2)}) async-start(), calls=%async_computation.3 | async-start | bytes 1572864 | tf_op jit(solution)/shard_map/all_gather | solution.py:103
  8.6 49.8 %copy-start.3 = (bf16[1,256,1024]{1,2,0:T(8,128)(2,1)}, bf16[1,256,1024]{1,2,0:T(8,128)(2,1)S(1)}, u32[]{:S(2)}) copy-start(bf16[1,256,1024]{1,2,0:T(8,128)(2,1)S(1)} %copy.116) | copy-start | bytes 1572868
  9.4 13.6 %copy-start.62 = (f32[1024]{0:T(1024)}, f32[1024]{0:T(1024)S(1)}, u32[]{:S(2)}) copy-start(f32[1024]{0:T(1024)S(1)} %convert_element_type.237) | copy-start | bytes 12292
  9.5 13.5 %copy-start.64 = (f32[256]{0:T(256)}, f32[256]{0:T(256)S(1)}, u32[]{:S(2)}) copy-start(f32[256]{0:T(256)S(1)} %add_rsqrt_fusion.1) | copy-start | bytes 3076
  18.2 49.6 %all-gather.10.cloned.1.call-start = ((), (), s32[]{:S(2)}) async-start(), calls=%async_computation.9 | async-start | bytes 2621440 | tf_op jit(solution)/shard_map/all_gather | solution.py:88
  18.9 72.4 %all-gather.8.cloned.1.call-start = ((), (), s32[]{:S(2)}) async-start(), calls=%async_computation.4 | async-start | bytes 2621440 | tf_op jit(solution)/shard_map/all_gather | solution.py:128
  27.2 18.9 %copy-start.43 = (bf16[256,16,32]{0,2,1:T(8,128)(2,1)}, bf16[256,16,32]{0,2,1:T(8,128)(2,1)S(1)}, u32[]{:S(2)}) copy-start(bf16[256,16,32]{0,2,1:T(8,128)(2,1)S(1)} %get-tuple-element.57) | copy-start | bytes 786436
  27.2 18.9 %copy-start.61 = (pred[256,512]{0,1:T(8,128)(4,1)S(1)}, pred[256,512]{0,1:T(8,128)(4,1)}, u32[]{:S(2)}) copy-start(pred[256,512]{0,1:T(8,128)(4,1)} %broadcast_compare_fusion) | copy-start | bytes 393220
  61.5 117.4 %reduce-scatter.6.cloned.1.call-start = ((), (), s32[]{:S(2)}) async-start(), calls=%async_computation.6 | async-start | bytes 2949120 | tf_op jit(solution)/shard_map/reduce_scatter | solution.py:176
  77.7 13.7 %copy-start.59 = (bf16[1024,16]{0,1:T(8,128)(2,1)S(1)}, bf16[1024,16]{0,1:T(8,128)(2,1)}, u32[]{:S(2)}) copy-start(bf16[1024,16]{0,1:T(8,128)(2,1)} %param.23) | copy-start | bytes 98308
  106.3 10.5 %copy-start.78 = (bf16[1024,512]{0,1:T(8,128)(2,1)}, bf16[1024,512]{0,1:T(8,128)(2,1)S(1)}, u32[]{:S(2)}) copy-start(bf16[1024,512]{0,1:T(8,128)(2,1)S(1)} %get-tuple-element.45) | copy-start | bytes 3145732
  109.0 37.1 %copy-start.24 = (bf16[1024,512]{0,1:T(8,128)(2,1)}, bf16[1024,512]{0,1:T(8,128)(2,1)S(1)}, u32[]{:S(2)}) copy-start(bf16[1024,512]{0,1:T(8,128)(2,1)S(1)} %get-tuple-element.54) | copy-start | bytes 3145732
  112.5 11.4 %copy-start.73 = (bf16[1024,512]{0,1:T(8,128)(2,1)}, bf16[1024,512]{0,1:T(8,128)(2,1)S(1)}, u32[]{:S(2)}) copy-start(bf16[1024,512]{0,1:T(8,128)(2,1)S(1)} %get-tuple-element.51) | copy-start | bytes 3145732
  116.0 11.2 %copy-start.83 = (bf16[1024,512]{0,1:T(8,128)(2,1)}, bf16[1024,512]{0,1:T(8,128)(2,1)S(1)}, u32[]{:S(2)}) copy-start(bf16[1024,512]{0,1:T(8,128)(2,1)S(1)} %get-tuple-element.39) | copy-start | bytes 3145732
  116.0 14.7 %copy-start.74 = (bf16[1024,512]{0,1:T(8,128)(2,1)}, bf16[1024,512]{0,1:T(8,128)(2,1)S(1)}, u32[]{:S(2)}) copy-start(bf16[1024,512]{0,1:T(8,128)(2,1)S(1)} %get-tuple-element.49) | copy-start | bytes 3145732
  146.0 67.4 %reduce-scatter.4.cloned.1.call-start = ((), (), s32[]{:S(2)}) async-start(), calls=%async_computation.5 | async-start | bytes 2621440 | tf_op jit(solution)/shard_map/reduce_scatter | solution.py:177
  154.7 102.0 %reduce-scatter.8.cloned.1.call-start = ((), (), s32[]{:S(2)}) async-start(), calls=%async_computation.7 | async-start | bytes 1572864 | tf_op jit(solution)/shard_map/reduce_scatter | solution.py:206
  165.6 14.4 %copy-start.58 = (f32[1024,16]{0,1:T(8,128)S(1)}, f32[1024,16]{0,1:T(8,128)}, u32[]{:S(2)}) copy-start(f32[1024,16]{0,1:T(8,128)} %copy-done.57) | copy-start | bytes 196612
  165.6 15.4 %copy-start.9 = (f32[256,1024]{0,1:T(8,128)S(1)}, f32[256,1024]{0,1:T(8,128)}, u32[]{:S(2)}) copy-start(f32[256,1024]{0,1:T(8,128)} %copy-done.8) | copy-start | bytes 3145732
  165.6 15.4 %copy-start.60 = (bf16[1024,16]{0,1:T(8,128)(2,1)S(1)}, bf16[1024,16]{0,1:T(8,128)(2,1)}, u32[]{:S(2)}) copy-start(bf16[1024,16]{0,1:T(8,128)(2,1)} %param.23) | copy-start | bytes 98308
  236.3 184.9 %all-reduce.9.cloned.1.call-start = ((), (), s32[]{:S(2)}) async-start(), calls=%async_computation.10 | async-start | bytes 12582912 | tf_op jit(solution)/shard_map/psum | solution.py:240
  260.9 565.3 %all-reduce.11.cloned.1.call-start = ((), (), s32[]{:S(2)}) async-start(), calls=%async_computation.11 | async-start | bytes 25165824 | tf_op jit(solution)/shard_map/psum | solution.py:181
  279.6 672.0 %all-reduce.7.cloned.1.call-start = ((), (), s32[]{:S(2)}) async-start(), calls=%async_computation.8 | async-start | bytes 131072 | tf_op jit(solution)/shard_map/psum | solution.py:244
  (74 other events, 223.1 us)
Sparse Core Ops, SparseCore 0:
  18.3 23.4 all-gather.5
  43.3 22.9 all-gather.9
  68.5 22.8 all-gather.7
  146.2 32.6 reduce-scatter.5
  181.9 31.4 reduce-scatter.3
  236.4 20.3 reduce-scatter.7
  264.4 156.7 all-reduce.8
  426.4 399.7 all-reduce.10
  833.3 118.3 all-reduce.6
where the time goes:
time: 967 us; the launch traced here: 960 us
  waiting for transfers between devices  669 us (69%)
  matrix products  145 us (15%)
  other arithmetic  52.2 us (5%)
  blocking collectives  45.6 us (5%)
  local copies, waits for them, and re-layouts  31.9 us (3%)
  between operations  15.1 us (2%)
    psum x1, waiting for transfers between devices, body(): lax.psum(jnp.stack(g), ('context', 'dp')).astype(F32)  394 us
    psum x1, waiting for transfers between devices, body(): lax.psum((grad_gain_one, grad_gain_two, grad_router_w), everywhere)  110 us
    psum x1, waiting for transfers between devices, body(): lax.psum(tuple((g.astype(BF16) for g in (grad_query_w, grad_key_w, grad_v...  90.1 us
    dot_general x17, matrix products, dot_t(): lax.dot_general(a, b, (((1,), (1,)), ((), ())), preferred_element_type=F32)  47.2 us
    psum x1, blocking collectives, body(): lax.psum((grad_gain_one, grad_gain_two, grad_router_w), everywhere)  39.5 us
    dot_general x17, matrix products, dot(): return jnp.dot(a, b, preferred_element_type=F32)  37.3 us
    dot_general x17, matrix products, t_dot(): lax.dot_general(a, b, (((0,), (0,)), ((), ())), preferred_element_type=F32)  35.9 us
    reduce_scatter x1, waiting for transfers between devices, body(): lax.psum_scatter(partial_y.astype(BF16), 'expert', scatter_dimension=0, t...  30.9 us
  transfers between devices with their start and end apart: 9, of which 8 were waited for; matrix products, arithmetic and copies ran while one was open for 13% of the time, Pallas kernels for 0%

commit v1 on v0

--- a/solution.py
+++ b/solution.py
@@ -178,7 +178,8 @@
         partial_y.astype(BF16), "expert", scatter_dimension=0, tiled=True
     ).astype(F32)
     total_gate, total_up, total_down = (
-        lax.psum(jnp.stack(g), ("context", "dp")).astype(F32) for g in (g_gate, g_up, g_down)
+        jnp.sum(lax.all_gather(jnp.stack(g), ("context", "dp")), axis=0).astype(F32)
+        for g in (g_gate, g_up, g_down)
     )
     outputs = (y_one + y_two).astype(BF16)[None]
     grad_final = cotangent[0].astype(F32)

time: 967 us -> 2490 us (2.57)
  waiting for transfers between devices: 669 us -> 2140 us
  other arithmetic: 52.2 us -> 102 us
    all_gather x0 -> x3, waiting for transfers between devices: none -> 1870 us  [body(): lax.all_gather(jnp.stack(g), ('context', 'dp'))]
    psum x1 -> x0, waiting for transfers between devices: 394 us -> none  [body(): lax.psum(jnp.stack(g), ('context', 'dp')).astype(F32)]
    reduce_sum x0 -> x3, other arithmetic: none -> 43.5 us  [body(): jnp.sum(lax.all_gather(jnp.stack(g), ('context', 'dp')), axis=0).astype(F32)]
  transfers between devices with their start and end apart: 9 -> 11, of which waited for: 8 -> 10; matrix products, arithmetic and copies ran while one was open for 13% -> 7% of each run, Pallas kernels for 0% -> 0%
where the time goes in v1:
time: 2490 us; the launch traced here: 2480 us
  waiting for transfers between devices  2140 us (86%)
  matrix products  146 us (6%)
  other arithmetic  102 us (4%)
  blocking collectives  45.8 us (2%)
  local copies, waits for them, and re-layouts  28.5 us (1%)
    all_gather x3, waiting for transfers between devices, body(): lax.all_gather(jnp.stack(g), ('context', 'dp'))  1870 us
    psum x1, waiting for transfers between devices, body(): lax.psum((grad_gain_one, grad_gain_two, grad_router_w), everywhere)  106 us
    psum x1, waiting for transfers between devices, body(): lax.psum(tuple((g.astype(BF16) for g in (grad_query_w, grad_key_w, grad_v...  79.8 us
    dot_general x17, matrix products, dot_t(): lax.dot_general(a, b, (((1,), (1,)), ((), ())), preferred_element_type=F32)  52 us
  transfers between devices with their start and end apart: 11, of which 10 were waited for; matrix products, arithmetic and copies ran while one was open for 7% of the time, Pallas kernels for 0%

profile of v1, /device:TPU:1, one launch (start us, length us, event | category | flops | bytes accessed | tf_op | source)
XLA Modules:
  0.0 2482.8 jit_solution(3626096376444910435)
XLA Ops:
  27.1 14.6 all-gather.12.cloned.1.call-done
  46.0 7.3 fusion.203
  60.9 6.1 all-gather
  67.1 4.6 fusion.16
  79.6 11.8 all-gather.14.cloned.1.call-done
  135.0 9.9 add_convert_fusion
  144.9 4.6 maximum_maximum_fusion
  161.1 21.3 reduce-scatter.6.cloned.1.call-done
  187.8 29.1 %reduce-scatter.4.cloned.1.call-done = bf16[256,1024]{0,1:T(8,128)(2,1)} async-done(((bf16[1024,1024]{0,1:T(8,128)(2,1)}), bf16[256,1024]{0,1:T(8,128)(2,1)}) %reduce-scatter.4.cloned.1.call-update) | async-done | bytes 524304 | tf_op jit(solution)/shard_map/reduce_scatter | solution.py:177
  223.7 4.9 fusion.1
  228.6 4.8 fusion.78
  248.4 13.1 reduce-scatter.8.cloned.1.call-done
  306.9 39.7 %all-reduce = (f32[1024]{0:T(1024)}, f32[1024]{0:T(1024)}) all-reduce(f32[1024]{0:T(1024)S(1)} %get-tuple-element.26, f32[1024]{0:T(1024)S(1)} %copy-done.41), channel_id=1, replica_groups=mesh['expert'=4,'context'=2,'dp'=4] {'expert','context','dp'}, use_global_device_ids=true, to_apply=%region_21.22 | all-reduce | flops 2048 | bytes 16384 | tf_op jit(solution)/shard_map/psum | solution.py:245
  346.5 79.8 %all-reduce.7.cloned.1.call-done = (bf16[1024,1024]{1,0:T(8,128)(2,1)}, bf16[1024,512]{1,0:T(8,128)(2,1)}, bf16[1024,512]{1,0:T(8,128)(2,1)}, bf16[1024,1024]{1,0:T(8,128)(2,1)}) async-done(((bf16[1024,1024]{1,0:T(8,128)(2,1)}, bf16[1024,512]{1,0:T(8,128)(2,1)}, bf16[1024,512]{1,0:T(8,128)(2,1)}, bf16[1024,1024]{1,0:T(8,128)(2,1)}), (bf16[1024,1024]{1,0:T(8,128)(2,1)}, bf16[1024,512]{1,0:T(8,128)(2,1)}, ...) | async-done | bytes 6291472 | tf_op jit(solution)/shard_map/psum | solution.py:241
  437.0 629.4 %all-gather.18.cloned.1.call-done = bf16[32,1024,512]{2,1,0:T(8,128)(2,1)} async-done(((bf16[4,1024,512]{2,1,0:T(8,128)(2,1)}), bf16[32,1024,512]{2,1,0:T(8,128)(2,1)}) %all-gather.18.cloned.1.call-update) | async-done | bytes 33554448 | tf_op jit(solution)/shard_map/all_gather | solution.py:181
  1066.4 14.5 reduce_sum.196
  1081.0 6.8 convert_element_type.297
  1087.7 619.7 %all-gather.20.cloned.1.call-done = bf16[32,1024,512]{2,1,0:T(8,128)(2,1)} async-done(((bf16[4,1024,512]{2,1,0:T(8,128)(2,1)}), bf16[32,1024,512]{2,1,0:T(8,128)(2,1)}) %all-gather.20.cloned.1.call-update) | async-done | bytes 33554448 | tf_op jit(solution)/shard_map/all_gather | solution.py:181
  1707.5 14.8 reduce_sum.197
  1722.2 6.8 convert_element_type.302
  1729.0 618.8 %all-gather.22.cloned.1.call-done = bf16[32,512,1024]{2,1,0:T(8,128)(2,1)} async-done(((bf16[4,512,1024]{2,1,0:T(8,128)(2,1)}), bf16[32,512,1024]{2,1,0:T(8,128)(2,1)}) %all-gather.22.cloned.1.call-update) | async-done | bytes 33554448 | tf_op jit(solution)/shard_map/all_gather | solution.py:181
  2347.8 14.2 reduce_sum.198
  2362.0 6.8 convert_element_type.307
  2368.8 105.7 %all-reduce.5.cloned.1.call-done = f32[1024,16]{0,1:T(8,128)} async-done(((f32[1024,16]{0,1:T(8,128)}), f32[1024,16]{0,1:T(8,128)}) %all-reduce.5.cloned.1.call-update) | async-done | bytes 65552 | tf_op jit(solution)/shard_map/psum | solution.py:245
  (270 shorter events, 178.5 us)
Async XLA Ops:
  7.2 50.6 %copy-start = (bf16[1024,1024]{1,0:T(8,128)(2,1)S(1)}, bf16[1024,1024]{1,0:T(8,128)(2,1)}, u32[]{:S(2)}) copy-start(bf16[1024,1024]{1,0:T(8,128)(2,1)} %param.21) | copy-start | bytes 6291460
  7.2 34.5 %all-gather.12.cloned.1.call-start = ((), (), s32[]{:S(2)}) async-start(), calls=%async_computation.3 | async-start | bytes 1572864 | tf_op jit(solution)/shard_map/all_gather | solution.py:103
  18.1 49.0 %all-gather.16.cloned.1.call-start = ((), (), s32[]{:S(2)}) async-start(), calls=%async_computation.9 | async-start | bytes 2621440 | tf_op jit(solution)/shard_map/all_gather | solution.py:88
  18.9 72.5 %all-gather.14.cloned.1.call-start = ((), (), s32[]{:S(2)}) async-start(), calls=%async_computation.4 | async-start | bytes 2621440 | tf_op jit(solution)/shard_map/all_gather | solution.py:128
  60.7 121.6 %reduce-scatter.6.cloned.1.call-start = ((), (), s32[]{:S(2)}) async-start(), calls=%async_computation.6 | async-start | bytes 2949120 | tf_op jit(solution)/shard_map/reduce_scatter | solution.py:176
  77.0 14.4 copy-start.35
  105.3 10.6 copy-start.56
  105.3 29.7 %copy-start.23 = (bf16[1024,512]{0,1:T(8,128)(2,1)}, bf16[1024,512]{0,1:T(8,128)(2,1)S(1)}, u32[]{:S(2)}) copy-start(bf16[1024,512]{0,1:T(8,128)(2,1)S(1)} %get-tuple-element.44) | copy-start | bytes 3145732
  109.0 8.2 copy-start.57
  109.0 9.5 copy-start.50
  112.4 9.3 copy-start.59
  112.4 12.6 copy-start.52
  115.9 12.4 copy-start.61
  115.9 15.9 copy-start.54
  149.6 67.4 %reduce-scatter.4.cloned.1.call-start = ((), (), s32[]{:S(2)}) async-start(), calls=%async_computation.5 | async-start | bytes 2621440 | tf_op jit(solution)/shard_map/reduce_scatter | solution.py:177
  158.6 26.0 %copy-start.36 = (bf16[1024,16]{0,1:T(8,128)(2,1)S(1)}, bf16[1024,16]{0,1:T(8,128)(2,1)}, u32[]{:S(2)}) copy-start(bf16[1024,16]{0,1:T(8,128)(2,1)} %param.23) | copy-start | bytes 98308
  158.6 26.0 %copy-start.40 = (f32[256]{0:T(256)S(1)}, f32[256]{0:T(256)}, u32[]{:S(2)}) copy-start(f32[256]{0:T(256)} %copy-done.39) | copy-start | bytes 3076
  158.6 102.9 %reduce-scatter.8.cloned.1.call-start = ((), (), s32[]{:S(2)}) async-start(), calls=%async_computation.7 | async-start | bytes 1572864 | tf_op jit(solution)/shard_map/reduce_scatter | solution.py:207
  241.0 185.4 %all-reduce.7.cloned.1.call-start = ((), (), s32[]{:S(2)}) async-start(), calls=%async_computation.13 | async-start | bytes 12582912 | tf_op jit(solution)/shard_map/psum | solution.py:241
  265.5 800.9 %all-gather.18.cloned.1.call-start = ((), (), s32[]{:S(2)}) async-start(), calls=%async_computation.10 | async-start | bytes 37748736 | tf_op jit(solution)/shard_map/all_gather | solution.py:181
  275.3 1432.1 %all-gather.20.cloned.1.call-start = ((), (), s32[]{:S(2)}) async-start(), calls=%async_computation.11 | async-start | bytes 37748736 | tf_op jit(solution)/shard_map/all_gather | solution.py:181
  286.2 2061.7 %all-gather.22.cloned.1.call-start = ((), (), s32[]{:S(2)}) async-start(), calls=%async_computation.12 | async-start | bytes 37748736 | tf_op jit(solution)/shard_map/all_gather | solution.py:181
  296.1 2178.4 %all-reduce.5.cloned.1.call-start = ((), (), s32[]{:S(2)}) async-start(), calls=%async_computation.8 | async-start | bytes 131072 | tf_op jit(solution)/shard_map/psum | solution.py:245
  2362.0 114.0 %copy-start.1 = (bf16[1024,1024]{1,0:T(8,128)(2,1)S(1)}, bf16[1024,1024]{1,0:T(8,128)(2,1)}, u32[]{:S(2)}) copy-start(bf16[1024,1024]{1,0:T(8,128)(2,1)} %param.21) | copy-start | bytes 6291460
  (54 other events, 138.5 us)
Sparse Core Ops, SparseCore 0:
  18.3 23.4 all-gather.11
  43.3 22.9 all-gather.15
  68.4 22.9 all-gather.13
  149.7 32.6 reduce-scatter.5
  185.5 31.4 reduce-scatter.3
  241.1 20.3 reduce-scatter.7
  269.7 156.6 all-reduce.6
  428.5 637.8 all-gather.17
  1068.5 638.9 all-gather.19
  1708.9 638.9 all-gather.21
  2354.0 120.4 all-reduce.4
